TPU v7x, 256 devices: a whole 4x4x8 slice. The times are simulated.
256 devices in a mesh: band: 8 (over x, y_lo), fft: 32 (over z, y_hi, core).
Axes of the slice: x: 4, y: 4 (y_hi: 2, y_lo: 2; y = y_hi * 2 + y_lo), z: 8, core: 2. Of those that a mesh axis runs over, the one named last changes fastest.
Arguments:
- orbitals: float32 [8, 256, 256, 256], P('band', 'fft'), may hold values from -6 to 6
- band_ids: int32 [8], replicated, may hold values from 0 to 7, each once
- owners: int32 [2], replicated, may hold values from 0 to 7, as said below
Outputs:
- exchange_potential: float32 [8, 256, 256, 256], P('band', 'fft')
Inputs may be any that keep to these rules, and one draw needn't show every extreme that they name: `band_ids`: each band number stands in exactly one slot; slot s belongs to band group s. `owners`: 2 different band numbers, one of which is 7.
All inputs are finite; a program needn't handle non-finite values.
Results may differ from a plain program's by a relative error of at most 0.0003.
Values sent between devices are 32-bit elements; how exact they have to be, the bound alone decides.
A program may use at most 64 MiB of HBM per device.

v0:
```python
import math

import jax
import jax.numpy as jnp
from jax import lax
from jax.sharding import PartitionSpec as P

cell_length = 46.9
highest = lax.Precision.HIGHEST


def broadcast(value, axis, source):
    kept = jnp.where(lax.axis_index(axis) == source, value, 0).astype(value.dtype)
    return lax.psum(kept, axis)


def cas_matrix(points, freq_list):
    positions = jnp.arange(points, dtype=jnp.int32)
    product = positions[:, None] * freq_list[None, :] % points
    angles = product.astype(jnp.float32) * (2.0 * math.pi / points)
    return jnp.cos(angles) + jnp.sin(angles)


def centred(freq_list, points):
    return jnp.where(freq_list < points // 2, freq_list, freq_list - points)


def coulomb_block(freq_x, freq_y, freq_z, points):
    wave_x = centred(freq_x, points)
    wave_y = centred(freq_y, points)
    wave_z = centred(freq_z, points)
    square_sum = (
        wave_x[:, None, None] ** 2 + wave_y[None, :, None] ** 2 + wave_z[None, None, :] ** 2
    )
    inside = (square_sum > 0) & (square_sum < (points // 4) ** 2)
    safe_sum = jnp.where(inside, square_sum, 1).astype(jnp.float32)
    weights = jnp.where(inside, cell_length**2 / math.pi / safe_sum, jnp.float32(0.0))
    return weights / float(points) ** 3


def per_device(orbitals, band_ids, owners):
    slot_count = orbitals.shape[0]
    planes = orbitals.shape[1]
    points = orbitals.shape[2]
    owner_count = owners.shape[0]
    all_slots = band_ids.shape[0]
    matches = band_ids[:, None] == owners[None, :]
    slot_ids = jnp.sum(
        jnp.where(matches, jnp.arange(all_slots, dtype=jnp.int32)[:, None], 0), axis=0
    )
    root_ids = slot_ids // slot_count
    local_slots = slot_ids % slot_count
    picked = jnp.take(orbitals, local_slots, axis=0)
    shared = []
    for owner_index in range(owner_count):
        shared.append(broadcast(picked[owner_index], "band", root_ids[owner_index]))
    owner_orbitals = jnp.stack(shared)
    density = (owner_orbitals[:, None] * orbitals[None, :]).reshape(
        owner_count * slot_count, planes, points, points
    )
    freq_list = jnp.arange(points, dtype=jnp.int32)
    cas_rows = cas_matrix(points, freq_list)
    spectrum = jnp.einsum("pxyz,zk->pxyk", density, cas_rows, precision=highest)
    spectrum = jnp.einsum("pxyk,yj->pxjk", spectrum, cas_rows, precision=highest)
    column_count = freq_list.shape[0] // lax.axis_size("fft")
    first_col = lax.axis_index("fft") * column_count
    freq_cols = lax.dynamic_slice_in_dim(freq_list, first_col, column_count)
    kernel = coulomb_block(freq_list, freq_cols, freq_list, points)
    coeffs = jnp.einsum(
        "pxjk,xi->pijk",
        lax.all_to_all(spectrum, "fft", split_axis=2, concat_axis=1, tiled=True),
        cas_rows,
        precision=highest,
    )
    coeffs = coeffs * kernel[None]
    restored = jnp.einsum("pijk,xi->pxjk", coeffs, cas_rows, precision=highest)
    returned = lax.all_to_all(restored, "fft", split_axis=1, concat_axis=2, tiled=True)
    potential = jnp.einsum("pxjk,yj->pxyk", returned, cas_rows, precision=highest)
    potential = jnp.einsum("pxyk,zk->pxyz", potential, cas_rows, precision=highest)
    potential = potential.reshape(owner_count, slot_count, planes, points, points)
    return -jnp.sum(owner_orbitals[:, None] * potential, axis=0)


def solution(mesh):
    placed = (P("band", "fft", None, None), P(), P())
    return jax.shard_map(
        per_device,
        mesh=mesh,
        in_specs=placed,
        out_specs=P("band", "fft", None, None),
        check_vma=False,
    )
```

profile of v0, /device:TPU:4, one launch (start us, length us, event | category | flops | bytes accessed | tf_op | source)
XLA Modules:
  0.0 466.3 jit_solution(17096257844778624435)
XLA Ops:
  6.5 0.0 all-reduce.3.cloned.1.call-start
  6.5 0.9 fusion.36
  7.4 0.6 fusion.63
  9.3 4.1 broadcast_select_fusion
  13.3 0.0 all-reduce.3.cloned.1.call-update
  13.3 192.2 %all-reduce.3.cloned.1.call-done = (f32[1,8,256,256]{3,2,1,0:T(8,128)}, f32[1,8,256,256]{3,2,1,0:T(8,128)}) async-done(((f32[1,8,256,256]{3,2,1,0:T(8,128)}, f32[1,8,256,256]{3,2,1,0:T(8,128)}), (f32[1,8,256,256]{3,2,1,0:T(8,128)}, f32[1,8,256,256]{3,2,1,0:T(8,128)})) %all-reduce.3.cloned.1.call-update) | async-done | bytes 4194320 | tf_op jit(solution)/shard_map/psum | solution.py:14
  205.5 0.0 copy-start.3
  205.5 0.0 copy-start.2
  205.5 2.0 constant_dynamic-update-slice_fusion.1
  207.5 0.2 copy-done.3
  207.7 0.1 constant_dynamic-update-slice_fusion
  207.9 0.0 copy-start
  207.9 0.5 copy-done.2
  208.4 4.5 fusion.10
  212.9 0.0 copy-done
  212.9 4.8 %convolution_bitcast_fusion = f32[2,8,256,256]{3,2,1,0:T(8,128)S(1)} fusion(f32[2,8,256,256]{3,2,1,0:T(8,128)S(1)} %fusion.10), kind=kOutput, calls=%fused_computation.16 | convolution fusion | flops 3222208512 | bytes 8388608 | tf_op jit(solution)/shard_map/pxyk,yj->pxjk/dot_general | solution.py:64
  217.7 4.5 copy.23
  222.3 9.7 %all-to-all-start = ((f32[2,8,256,256]{3,1,0,2:T(8,128)}), f32[2,8,256,256]{3,1,0,2:T(8,128)}, u32[]{:S(2)}, u32[]{:S(2)}) async-start(f32[2,8,256,256]{3,1,0,2:T(8,128)} %copy.23), calls=%async_computation | async-start | bytes 8388608 | tf_op jit(solution)/shard_map/all_to_all | solution.py:71
  232.0 0.1 fusion.38
  232.1 0.1 broadcast_add_fusion
  232.1 0.7 fusion.20
  232.8 95.8 %all-to-all-done = f32[2,8,256,256]{3,1,0,2:T(8,128)} async-done(((f32[2,8,256,256]{3,1,0,2:T(8,128)}), f32[2,8,256,256]{3,1,0,2:T(8,128)}, u32[]{:S(2)}, u32[]{:S(2)}) %all-to-all-start) | async-done | bytes 4194336 | tf_op jit(solution)/shard_map/all_to_all | solution.py:71
  328.6 4.6 copy.25
  333.3 5.7 %fusion.7 = f32[256,2,8,256]{3,0,2,1:T(8,128)S(1)} fusion(f32[2,256,8,256]{3,2,1,0:T(8,128)S(1)} %bitcast.48), kind=kOutput, calls=%fused_computation.7 | convolution fusion | flops 3222208512 | bytes 8388608 | tf_op jit(solution)/shard_map/pxjk,xi->pijk/dot_general | solution.py:69
  339.0 5.1 %fusion.12 = f32[2,256,8,256]{3,1,2,0:T(8,128)S(1)} fusion(f32[256,2,8,256]{3,0,2,1:T(8,128)S(1)} %fusion.7, f32[256,8,256]{2,0,1:T(8,128)S(1)} %fusion.20), kind=kOutput, calls=%fused_computation.17 | convolution fusion | flops 3223257088 | bytes 10485760 | tf_op jit(solution)/shard_map/pijk,xi->pxjk/dot_general | solution.py:76
  344.1 2.4 copy.28
  346.6 101.1 %all_to_all.36 = f32[2,256,8,256]{3,2,0,1:T(8,128)S(1)} all-to-all(f32[2,256,8,256]{3,2,0,1:T(8,128)S(1)} %copy.28), channel_id=1, replica_groups=mesh['band'=8,'fft'=32] {'fft'}, dimensions={1} | all-to-all | bytes 8388608 | tf_op jit(solution)/shard_map/all_to_all | solution.py:77
  447.6 0.0 copy-start.1
  447.6 5.3 %fusion.2 = f32[256,2,8,256]{3,0,2,1:T(8,128)S(1)} fusion(f32[2,8,32,8,256]{4,3,0,1,2:T(8,128)S(1)} %bitcast.49), kind=kOutput, calls=%fused_computation.2 | convolution fusion | flops 3222208512 | bytes 8388608 | tf_op jit(solution)/shard_map/pxjk,yj->pxyk/dot_general | solution.py:78
  452.9 0.0 copy-done.1
  452.9 4.7 %multiply_reduce_fusion = f32[8,256,256]{2,1,0:T(8,128)S(1)} fusion(f32[2,8,256,256]{3,2,1,0:T(8,128)S(1)} %copy-done.1, f32[256,2,8,256]{3,0,2,1:T(8,128)S(1)} %fusion.2), kind=kOutput, calls=%fused_computation.9 | convolution fusion | flops 3223781376 | bytes 10485760 | tf_op jit(solution)/shard_map/pxyk,zk->pxyz/dot_general | solution.py:79
  457.6 1.5 negate_bitcast_fusion
  (2 shorter events, 0.0 us)
Async XLA Ops:
  6.5 199.0 %all-reduce.3.cloned.1.call-start = ((), (), s32[]{:S(2)}) async-start(), calls=%async_computation.2 | async-start | bytes 8388608 | tf_op jit(solution)/shard_map/psum | solution.py:14
  205.5 2.2 copy-start.3
  205.5 2.9 copy-start.2
  207.9 5.0 %copy-start = (f32[2,8,256,256]{3,2,1,0:T(8,128)}, f32[2,8,256,256]{3,2,1,0:T(8,128)S(1)}, u32[]{:S(2)}) copy-start(f32[2,8,256,256]{3,2,1,0:T(8,128)S(1)} %constant_dynamic-update-slice_fusion) | copy-start | bytes 12582916
  222.3 106.4 %all-to-all-start = ((f32[2,8,256,256]{3,1,0,2:T(8,128)}), f32[2,8,256,256]{3,1,0,2:T(8,128)}, u32[]{:S(2)}, u32[]{:S(2)}) async-start(f32[2,8,256,256]{3,1,0,2:T(8,128)} %copy.23), calls=%async_computation | async-start | bytes 8388608 | tf_op jit(solution)/shard_map/all_to_all | solution.py:71
  447.6 5.3 %copy-start.1 = (f32[2,8,256,256]{3,2,1,0:T(8,128)S(1)}, f32[2,8,256,256]{3,2,1,0:T(8,128)}, u32[]{:S(2)}) copy-start(f32[2,8,256,256]{3,2,1,0:T(8,128)} %copy-done) | copy-start | bytes 12582916
Sparse Core Ops, SparseCore 0:
  13.4 192.0 all-reduce.2
where the time goes:
time: 475 us; the launch traced here: 466 us
  waiting for transfers between devices  288 us (61%)
  blocking collectives  101 us (21%)
  matrix products  30.1 us (6%)
  between operations  15.2 us (3%)
  local copies, waits for them, and re-layouts  15 us (3%)
  starting transfers between devices  9.69 us (2%)
  other arithmetic  7.22 us (2%)
    psum x1, waiting for transfers between devices, broadcast(): return lax.psum(kept, axis)  192 us
    all_to_all x1, blocking collectives, per_device(): lax.all_to_all(restored, 'fft', split_axis=1, concat_axis=2, tiled=True)  101 us
    all_to_all x1, waiting for transfers between devices, per_device(): lax.all_to_all(spectrum, 'fft', split_axis=2, concat_axis=1, tiled=True)  95.8 us
    all_to_all x1, starting transfers between devices, per_device(): lax.all_to_all(spectrum, 'fft', split_axis=2, concat_axis=1, tiled=True)  9.68 us
  transfers between devices with their start and end apart: 2, of which 2 were waited for; matrix products, arithmetic and copies ran while one was open for 0% of the time, Pallas kernels for 0%

commit v1 on v0

--- a/solution.py
+++ b/solution.py
@@ -59,6 +59,8 @@
         owner_count * slot_count, planes, points, points
     )
     freq_list = jnp.arange(points, dtype=jnp.int32)
+    half = points // 2
+    freq_list = (freq_list[:half] - half // 2) % points
     cas_rows = cas_matrix(points, freq_list)
     spectrum = jnp.einsum("pxyz,zk->pxyk", density, cas_rows, precision=highest)
     spectrum = jnp.einsum("pxyk,yj->pxjk", spectrum, cas_rows, precision=highest)

time: 475 us -> 310 us (0.65)
  the two profiles are of different devices: /device:TPU:4 before, /device:TPU:1 now
where the time goes in v1:
time: 310 us; the launch traced here: 308 us
  waiting for transfers between devices  219 us (71%)
  blocking collectives  33.6 us (11%)
  matrix products  15.8 us (5%)
  between operations  14.7 us (5%)
  starting transfers between devices  10 us (3%)
  local copies, waits for them, and re-layouts  7.9 us (3%)
  other arithmetic  6.72 us (2%)
    psum x1, waiting for transfers between devices, broadcast(): return lax.psum(kept, axis)  192 us
    all_to_all x1, blocking collectives, per_device(): lax.all_to_all(restored, 'fft', split_axis=1, concat_axis=2, tiled=True)  33.6 us
    all_to_all x1, waiting for transfers between devices, per_device(): lax.all_to_all(spectrum, 'fft', split_axis=2, concat_axis=1, tiled=True)  27.8 us
    all_to_all x1, starting transfers between devices, per_device(): lax.all_to_all(spectrum, 'fft', split_axis=2, concat_axis=1, tiled=True)  10 us
  transfers between devices with their start and end apart: 2, of which 2 were waited for; matrix products, arithmetic and copies ran while one was open for 0% of the time, Pallas kernels for 0%

profile of v1, /device:TPU:1, one launch (start us, length us, event | category | flops | bytes accessed | tf_op | source)
XLA Modules:
  0.0 308.1 jit_solution(15491944150978100211)
XLA Ops:
  6.5 0.0 all-reduce.3.cloned.1.call-start
  6.5 0.9 fusion.26
  7.4 0.6 fusion.54
  9.2 4.0 %broadcast_select_fusion = (f32[1,8,256,256]{3,2,1,0:T(8,128)}, f32[1,8,256,256]{3,2,1,0:T(8,128)}) fusion(f32[1,8,256,256]{3,2,1,0:T(8,128)} %param.3, pred[]{:T(512)S(6)} %eq.29, pred[]{:T(512)S(6)} %eq.28), kind=kLoop, calls=%fused_computation.15 | loop fusion | flops 1048576 | bytes 6291458 | tf_op jit(solution)/shard_map/jit(_where)/select_n | solution.py:13
  13.2 0.0 all-reduce.3.cloned.1.call-update
  13.3 191.6 %all-reduce.3.cloned.1.call-done = (f32[1,8,256,256]{3,2,1,0:T(8,128)}, f32[1,8,256,256]{3,2,1,0:T(8,128)}) async-done(((f32[1,8,256,256]{3,2,1,0:T(8,128)}, f32[1,8,256,256]{3,2,1,0:T(8,128)}), (f32[1,8,256,256]{3,2,1,0:T(8,128)}, f32[1,8,256,256]{3,2,1,0:T(8,128)})) %all-reduce.3.cloned.1.call-update) | async-done | bytes 4194320 | tf_op jit(solution)/shard_map/psum | solution.py:14
  204.9 0.0 copy-start.3
  204.9 1.9 constant_dynamic-update-slice_fusion.1
  206.8 0.3 copy-done.3
  207.1 0.2 constant_dynamic-update-slice_fusion
  207.4 0.0 copy-start
  207.4 2.3 copy-done.2
  209.6 4.1 %fusion = f32[2,8,256,128]{3,2,1,0:T(8,128)S(1)} fusion(f32[2,8,256,256]{3,2,1,0:T(8,128)S(1)} %constant_dynamic-update-slice_fusion, f32[8,256,256]{2,1,0:T(8,128)S(1)} %bitcast.45, s32[128]{0:T(128)S(1)} %get-tuple-element.8), kind=kOutput, calls=%fused_computation.1 | convolution fusion | flops 1612152832 | bytes 8389120 | tf_op jit(solution)/shard_map/pxyz,zk->pxyk/dot_general | solution.py:65
  213.8 0.0 copy-done
  213.8 1.8 convolution_bitcast_fusion.1
  215.5 1.6 copy.23
  217.1 10.0 %all-to-all-start = ((f32[2,8,128,128]{3,1,0,2:T(8,128)}), f32[2,8,128,128]{3,1,0,2:T(8,128)S(1)}, u32[]{:S(2)}, u32[]{:S(2)}) async-start(f32[2,8,128,128]{3,1,0,2:T(8,128)} %copy.23), calls=%async_computation | async-start | bytes 2097152 | tf_op jit(solution)/shard_map/all_to_all | solution.py:73
  227.1 0.1 fusion.28
  227.2 0.1 broadcast_add_fusion
  227.3 0.2 fusion.12
  227.4 27.8 %all-to-all-done = f32[2,8,128,128]{3,1,0,2:T(8,128)S(1)} async-done(((f32[2,8,128,128]{3,1,0,2:T(8,128)}), f32[2,8,128,128]{3,1,0,2:T(8,128)S(1)}, u32[]{:S(2)}, u32[]{:S(2)}) %all-to-all-start) | async-done | bytes 1048608 | tf_op jit(solution)/shard_map/all_to_all | solution.py:73
  255.2 1.2 fusion.4
  256.5 1.5 convolution_bitcast_fusion
  258.0 0.7 copy.27
  258.7 33.6 %all_to_all.36 = f32[2,256,4,128]{3,2,0,1:T(4,128)S(1)} all-to-all(f32[2,256,4,128]{3,2,0,1:T(4,128)S(1)} %copy.27), channel_id=1, replica_groups=mesh['band'=8,'fft'=32] {'fft'}, dimensions={1} | all-to-all | bytes 2097152 | tf_op jit(solution)/shard_map/all_to_all | solution.py:79
  292.2 0.2 copy.44
  292.4 0.0 copy-start.1
  292.5 0.1 copy.29
  292.6 2.4 fusion.7
  295.0 0.0 copy-done.1
  295.0 4.8 %multiply_reduce_fusion = f32[8,256,256]{2,1,0:T(8,128)S(1)} fusion(f32[2,8,256,256]{3,2,1,0:T(8,128)S(1)} %copy-done.1, f32[256,2,8,128]{3,0,2,1:T(8,128)S(1)} %fusion.7, s32[128]{0:T(128)S(1)} %get-tuple-element.8), kind=kOutput, calls=%fused_computation | convolution fusion | flops 1612677120 | bytes 8389120 | tf_op jit(solution)/shard_map/pxyk,zk->pxyz/dot_general | solution.py:81
  299.8 1.5 negate_bitcast_fusion
  (3 shorter events, 0.0 us)
Async XLA Ops:
  6.5 198.4 %all-reduce.3.cloned.1.call-start = ((), (), s32[]{:S(2)}) async-start(), calls=%async_computation.2 | async-start | bytes 8388608 | tf_op jit(solution)/shard_map/psum | solution.py:14
  204.9 2.2 copy-start.3
  207.1 2.5 copy-start.2
  207.4 6.4 %copy-start = (f32[2,8,256,256]{3,2,1,0:T(8,128)}, f32[2,8,256,256]{3,2,1,0:T(8,128)S(1)}, u32[]{:S(2)}) copy-start(f32[2,8,256,256]{3,2,1,0:T(8,128)S(1)} %constant_dynamic-update-slice_fusion) | copy-start | bytes 12582916
  217.1 38.1 %all-to-all-start = ((f32[2,8,128,128]{3,1,0,2:T(8,128)}), f32[2,8,128,128]{3,1,0,2:T(8,128)S(1)}, u32[]{:S(2)}, u32[]{:S(2)}) async-start(f32[2,8,128,128]{3,1,0,2:T(8,128)} %copy.23), calls=%async_computation | async-start | bytes 2097152 | tf_op jit(solution)/shard_map/all_to_all | solution.py:73
  292.4 2.5 copy-start.1
Sparse Core Ops, SparseCore 0:
  13.4 191.4 all-reduce.2
